TPU v7x, 128 devices: a whole 4x4x4 slice. The times are simulated.
128 devices in a mesh: dp: 16 (over x, z), section: 8 (over y, core).
Axes of the slice: x: 4, y: 4, z: 4, core: 2. Of those that a mesh axis runs over, the one named last changes fastest.
Arguments:
- acts: bfloat16 [8, 128, 6144], P('section', None, 'dp'), may hold values from -6 to 6
- grad_top: bfloat16 [128, 6144], P(None, 'dp'), may hold values from -6 to 6
- weights_t: bfloat16 [8, 6144, 6144], P('section', 'dp'), may hold values from -0.078125 to 0.078125
- slopes: bfloat16 [8, 128, 6144], P('section', None, 'dp'), may hold values from 0.19921875 to 1.59375
- running: float32 [8, 24, 512, 512], P('section', None, 'dp'), as said below
- ns_counts: int32 [8, 24], P('section'), may hold values from 1 to 2
- assignment: int32 [8, 24], P('section'), may hold values from 0 to 15, as said below
Outputs:
- backs: bfloat16 [8, 128, 6144], P('section', None, 'dp')
- precond_acts: bfloat16 [8, 128, 6144], P('section', None, 'dp')
- precond_grads: bfloat16 [8, 128, 6144], P('section', None, 'dp')
- inverses: bfloat16 [8, 16, 3, 512, 512], P('section', 'dp')
Inputs may be any that keep to these rules, and one draw needn't show every extreme that they name: `assignment`: each tile of a layer names the dp index that owns it. No owner holds more than 3 tiles of one layer, and in every layer one owner holds exactly 3. `running`: every tile is symmetric.
All inputs are finite; a program needn't handle non-finite values. Where the computation divides by a largest or mean magnitude, that divisor is 1e-20 or more.
Results may differ from a plain program's by a relative error of at most 0.035.
Values may be sent and summed in bfloat16 or wider, within the bound.
A program may use at most 64 MiB of HBM per device.

v0:
```python
import jax
import jax.numpy as jnp
from jax import lax
from jax.sharding import PartitionSpec as P

BLOCK = 512
ROWS = 128
MOST = 3
NBLK = 12
TILES = 24


DECAY = 0.8
DAMP = 0.1


def from_behind(block, axis, distance):
    devices = range(lax.axis_size(axis))
    route = [(i - distance, i) for i in devices if i - distance in devices]
    return lax.ppermute(block, axis, route)


def shards(acts, grad_top, weights_t, slopes, running, ns_counts, assignment):
    section_count = lax.axis_size("section")
    section_id = lax.axis_index("section")
    dp_count = lax.axis_size("dp")
    my_index = lax.axis_index("dp")
    acts_local = acts[0]
    weight_rows = weights_t[0]
    slope_local = slopes[0].astype(jnp.float32)
    row_total = acts_local.shape[0]
    width_local = acts_local.shape[1]
    incoming = grad_top
    backs = jnp.zeros_like(grad_top)
    out_grads = jnp.zeros_like(grad_top)
    for step in range(section_count):
        is_here = section_id == section_count - 1 - step
        summed = lax.psum_scatter(
            jnp.dot(incoming, weight_rows, preferred_element_type=jnp.float32).astype(jnp.bfloat16),
            "dp",
            scatter_dimension=1,
            tiled=True,
        ).astype(jnp.float32)
        backward = (summed * slope_local).astype(jnp.bfloat16)
        backs = jnp.where(is_here, backward, backs)
        out_grads = jnp.where(is_here, incoming, out_grads)
        if step + 1 < section_count:
            incoming = from_behind(backward, "section", -1)
    acts_full, grads_full = (
        lax.all_gather(acts_local, "dp", axis=1, tiled=True),
        lax.all_gather(out_grads, "dp", axis=1, tiled=True),
    )
    rows_each = BLOCK // dp_count
    tile_ids = jnp.arange(TILES, dtype=jnp.int32)

    def own_rows(full):
        shaped = full.reshape(row_total, NBLK, BLOCK)
        mine = lax.dynamic_slice_in_dim(shaped, my_index * rows_each, rows_each, 2)
        return jnp.einsum("rtp,rtc->tpc", mine, shaped, preferred_element_type=jnp.float32)

    fresh = jnp.concatenate([own_rows(acts_full), own_rows(grads_full)], axis=0)
    column_iota = lax.broadcasted_iota(jnp.int32, (rows_each, BLOCK), 1)
    row_iota = lax.broadcasted_iota(jnp.int32, (rows_each, BLOCK), 0)
    ident_rows = (column_iota == row_iota + my_index * rows_each).astype(jnp.float32)
    factor_rows = DECAY * running[0] + (1.0 - DECAY) * (fresh / ROWS) + DAMP * ident_rows
    owners = assignment[0]
    matches = (owners[:, None] == owners[None, :]) & (tile_ids[None, :] < tile_ids[:, None])
    slots_of = jnp.sum(matches.astype(jnp.int32), axis=1)
    outbox = (
        jnp.zeros((dp_count, MOST, rows_each, BLOCK), jnp.float32)
        .at[owners, slots_of]
        .set(factor_rows)
    )
    inbox = lax.all_to_all(
        outbox.astype(jnp.bfloat16), "dp", split_axis=0, concat_axis=2, tiled=True
    ).astype(outbox.dtype)
    held = (
        (owners == my_index)[:, None]
        & (slots_of[:, None] == jnp.arange(MOST, dtype=jnp.int32)[None, :])
    ).astype(jnp.int32)
    filled = jnp.sum(held, axis=0) > 0
    tile_of = jnp.sum(held * tile_ids[:, None], axis=0)
    step_counts = jnp.sum(held * ns_counts[0][:, None], axis=0)
    ident = jnp.eye(BLOCK, dtype=jnp.float32)
    factor = jnp.where(filled[:, None, None], inbox[0], ident)
    scales = jnp.max(jnp.sum(jnp.abs(factor), axis=2), axis=1)[:, None, None]
    iterate = (2.0 * ident - factor / scales) / scales
    factor_b = factor.astype(jnp.bfloat16)
    iterate_b = iterate.astype(jnp.bfloat16)
    product = jnp.einsum("mij,mjk->mik", factor_b, iterate_b, preferred_element_type=jnp.float32)
    remainder = (2.0 * ident - product).astype(jnp.bfloat16)
    advanced = jnp.einsum("mij,mjk->mik", iterate_b, remainder, preferred_element_type=jnp.float32)
    iterate = jnp.where((step_counts > 1)[:, None, None], advanced, iterate)
    inverse_b = iterate.astype(jnp.bfloat16)
    inverses = jnp.where(filled[:, None, None], inverse_b, jnp.zeros_like(inverse_b))
    slot_results = []
    kinds = []
    block_ids = []
    for m in range(MOST):
        is_grad = (tile_of[m] >= NBLK).astype(jnp.int32)
        block_id = tile_of[m] % NBLK
        source = jnp.where(is_grad > 0, grads_full, acts_full)
        columns = lax.dynamic_slice_in_dim(source, block_id * BLOCK, BLOCK, 1)
        slot_results.append(
            jnp.dot(columns, inverse_b[m], preferred_element_type=jnp.float32).astype(jnp.bfloat16)
        )
        kinds.append(is_grad)
        block_ids.append(block_id)
    stacked = jnp.stack(slot_results)
    gathered = lax.all_gather(stacked, "dp", axis=0, tiled=True)
    picked = jnp.take(gathered, owners * MOST + slots_of, axis=0)

    def own_columns(tiles):
        whole = tiles.transpose(1, 0, 2).reshape(row_total, NBLK * BLOCK)
        return lax.dynamic_slice_in_dim(whole, my_index * width_local, width_local, 1)

    pre_acts = own_columns(picked[:NBLK])
    pre_grads = own_columns(picked[NBLK:])
    return (backs[None], pre_acts[None], pre_grads[None], inverses[None, None])


def solution(mesh):
    in_specs = (
        P("section", None, "dp"),
        P(None, "dp"),
        P("section", "dp", None),
        P("section", None, "dp"),
        P("section", None, "dp", None),
        P("section", None),
        P("section", None),
    )
    out_specs = (
        P("section", None, "dp"),
        P("section", None, "dp"),
        P("section", None, "dp"),
        P("section", "dp", None, None, None),
    )
    return jax.shard_map(shards, mesh=mesh, in_specs=in_specs, out_specs=out_specs, check_vma=False)
```

profile of v0, /device:TPU:0, one launch (start us, length us, event | category | flops | bytes accessed | tf_op | source)
XLA Modules:
  0.0 862.6 jit_solution(2374835030588546242)
XLA Ops:
  7.2 3.4 convolution_convert_fusion.7
  13.2 75.5 %reduce-scatter.25.cloned.1.call-done = bf16[384,128]{1,0:T(8,128)(2,1)} async-done(((bf16[6144,128]{1,0:T(8,128)(2,1)}), bf16[384,128]{1,0:T(8,128)(2,1)}) %reduce-scatter.25.cloned.1.call-update) | async-done | bytes 98320
  90.9 1.9 collective-permute-done
  92.8 3.3 convolution_convert_fusion.6
  97.8 74.9 %reduce-scatter.27.cloned.1.call-done = bf16[384,128]{1,0:T(8,128)(2,1)} async-done(((bf16[6144,128]{1,0:T(8,128)(2,1)}), bf16[384,128]{1,0:T(8,128)(2,1)}) %reduce-scatter.27.cloned.1.call-update) | async-done | bytes 98320
  174.9 1.9 collective-permute-done.1
  176.8 3.4 convolution_convert_fusion.5
  181.8 75.0 %reduce-scatter.29.cloned.1.call-done = bf16[384,128]{1,0:T(8,128)(2,1)} async-done(((bf16[6144,128]{1,0:T(8,128)(2,1)}), bf16[384,128]{1,0:T(8,128)(2,1)}) %reduce-scatter.29.cloned.1.call-update) | async-done | bytes 98320
  259.1 1.9 collective-permute-done.2
  261.0 3.4 convolution_convert_fusion.4
  266.0 75.0 %reduce-scatter.31.cloned.1.call-done = bf16[384,128]{1,0:T(8,128)(2,1)} async-done(((bf16[6144,128]{1,0:T(8,128)(2,1)}), bf16[384,128]{1,0:T(8,128)(2,1)}) %reduce-scatter.31.cloned.1.call-update) | async-done | bytes 98320
  343.2 1.9 collective-permute-done.3
  345.1 3.4 convolution_convert_fusion.3
  350.1 75.0 %reduce-scatter.33.cloned.1.call-done = bf16[384,128]{1,0:T(8,128)(2,1)} async-done(((bf16[6144,128]{1,0:T(8,128)(2,1)}), bf16[384,128]{1,0:T(8,128)(2,1)}) %reduce-scatter.33.cloned.1.call-update) | async-done | bytes 98320
  427.4 1.9 collective-permute-done.4
  429.3 3.4 convolution_convert_fusion.2
  434.3 74.9 %reduce-scatter.35.cloned.1.call-done = bf16[384,128]{1,0:T(8,128)(2,1)} async-done(((bf16[6144,128]{1,0:T(8,128)(2,1)}), bf16[384,128]{1,0:T(8,128)(2,1)}) %reduce-scatter.35.cloned.1.call-update) | async-done | bytes 98320
  513.4 3.4 convolution_convert_fusion.1
  520.0 73.4 %reduce-scatter.37.cloned.1.call-done = bf16[384,128]{1,0:T(8,128)(2,1)} async-done(((bf16[6144,128]{1,0:T(8,128)(2,1)}), bf16[384,128]{1,0:T(8,128)(2,1)}) %reduce-scatter.37.cloned.1.call-update) | async-done | bytes 98320
  603.8 35.1 %all-gather.9.cloned.1.call-done = bf16[1,128,6144]{1,2,0:T(8,128)(2,1)} async-done(((bf16[1,128,384]{1,2,0:T(8,128)(2,1)}), bf16[1,128,6144]{1,2,0:T(8,128)(2,1)}) %all-gather.9.cloned.1.call-update) | async-done | bytes 1572880 | tf_op jit(solution)/shard_map/all_gather | solution.py:50
  638.9 2.1 fusion.42
  641.1 44.0 %all-gather.5.cloned.1.call-done = bf16[128,6144]{0,1:T(8,128)(2,1)} async-done(((bf16[128,384]{0,1:T(8,128)(2,1)}), bf16[128,6144]{0,1:T(8,128)(2,1)}) %all-gather.5.cloned.1.call-update) | async-done | bytes 1572880 | tf_op jit(solution)/shard_map/all_gather | solution.py:51
  685.0 2.1 fusion.40
  689.1 4.2 scatter_fusion
  694.7 4.9 all-to-all-start
  703.6 3.4 convolution_convert_fusion
  708.6 13.8 %all-to-all-done = bf16[16,3,32,512]{3,2,1,0:T(8,128)(2,1)S(1)} async-done(((bf16[16,3,32,512]{3,2,1,0:T(8,128)(2,1)}), bf16[16,3,32,512]{3,2,1,0:T(8,128)(2,1)S(1)}, u32[]{:S(2)}, u32[]{:S(2)}) %all-to-all-start) | async-done | bytes 1572896 | tf_op jit(solution)/shard_map/all_to_all | solution.py:74
  723.5 1.9 copy.99
  725.5 8.8 %select_convert_fusion = bf16[3,512,512]{2,1,0:T(8,128)(2,1)S(1)} fusion(pred[3]{0:T(512)(128)(4,1)S(1)} %copy-done.19, f32[3,512,512]{2,1,0:T(8,128)} %bitcast.136, f32[512,512]{1,0:T(8,128)S(1)} %copy-done.2, f32[512,512]{1,0:T(8,128)} %fusion.18, pred[3]{0:T(512)(128)(4,1)S(1)} %broadcast_compare_fusion, f32[3]{0:T(128)S(1)} %reduce_max.9), kind=kOutput, calls=%fused_computation.22 | convolution fusion | flops 1626341376 | bytes 6815762 | tf_op jit(solution)/shard_map/mij,mjk->mik/dot_general | solution.py:92
  739.1 45.0 %reduce-scatter.39.cloned.1.call-done = bf16[384,128]{1,0:T(8,128)(2,1)} async-done(((bf16[6144,128]{1,0:T(8,128)(2,1)}), bf16[384,128]{1,0:T(8,128)(2,1)}) %reduce-scatter.39.cloned.1.call-update) | async-done | bytes 98320
  787.1 59.8 %all-gather.7.cloned.1.call-done = bf16[48,128,512]{2,1,0:T(8,128)(2,1)} async-done(((bf16[3,128,512]{2,1,0:T(8,128)(2,1)}), bf16[48,128,512]{2,1,0:T(8,128)(2,1)}) %all-gather.7.cloned.1.call-update) | async-done | bytes 6291472 | tf_op jit(solution)/shard_map/all_gather | solution.py:110
  846.9 3.5 gather_fusion
  (124 shorter events, 58.8 us)
Async XLA Ops:
  7.2 81.5 %reduce-scatter.25.cloned.1.call-start = ((), (), s32[]{:S(2)}) async-start(), calls=%async_computation.12 | async-start | bytes 1671168
  12.2 160.5 %reduce-scatter.27.cloned.1.call-start = ((), (), s32[]{:S(2)}) async-start(), calls=%async_computation.13 | async-start | bytes 1671168
  89.6 3.2 collective-permute-start
  97.7 159.1 %reduce-scatter.29.cloned.1.call-start = ((), (), s32[]{:S(2)}) async-start(), calls=%async_computation.14 | async-start | bytes 1671168
  173.7 3.2 collective-permute-start.1
  181.8 159.2 %reduce-scatter.31.cloned.1.call-start = ((), (), s32[]{:S(2)}) async-start(), calls=%async_computation.15 | async-start | bytes 1671168
  257.8 3.2 collective-permute-start.2
  265.9 159.2 %reduce-scatter.33.cloned.1.call-start = ((), (), s32[]{:S(2)}) async-start(), calls=%async_computation.16 | async-start | bytes 1671168
  341.9 3.2 collective-permute-start.3
  350.1 159.2 %reduce-scatter.35.cloned.1.call-start = ((), (), s32[]{:S(2)}) async-start(), calls=%async_computation.17 | async-start | bytes 1671168
  426.1 6.6 copy-start.8
  426.1 3.2 collective-permute-start.4
  434.2 159.2 %reduce-scatter.37.cloned.1.call-start = ((), (), s32[]{:S(2)}) async-start(), calls=%async_computation.18 | async-start | bytes 1671168
  510.2 6.6 copy-start.10
  510.2 3.2 collective-permute-start.5
  518.3 77.5 %copy-start.3 = (bf16[128,384]{1,0:T(8,128)(2,1)S(1)}, bf16[128,384]{1,0:T(8,128)(2,1)}, u32[]{:S(2)}) copy-start(bf16[128,384]{1,0:T(8,128)(2,1)} %param.8) | copy-start | bytes 294916
  518.3 80.0 %copy-start.16 = (s32[1,24]{1,0:T(1,128)S(1)}, s32[1,24]{1,0:T(1,128)}, u32[]{:S(2)}) copy-start(s32[1,24]{1,0:T(1,128)} %param.13) | copy-start | bytes 292
  518.3 80.2 %copy-start.17 = (s32[1,24]{1,0:T(1,128)S(1)}, s32[1,24]{1,0:T(1,128)}, u32[]{:S(2)}) copy-start(s32[1,24]{1,0:T(1,128)} %param.12) | copy-start | bytes 292
  518.3 120.6 %all-gather.9.cloned.1.call-start = ((), (), s32[]{:S(2)}) async-start(), calls=%async_computation.11 | async-start | bytes 1671168 | tf_op jit(solution)/shard_map/all_gather | solution.py:50
  520.0 165.1 %all-gather.5.cloned.1.call-start = ((), (), s32[]{:S(2)}) async-start(), calls=%async_computation.9 | async-start | bytes 1671168 | tf_op jit(solution)/shard_map/all_gather | solution.py:51
  594.3 46.7 %copy-start.12 = (bf16[128,384]{0,1:T(8,128)(2,1)}, bf16[128,384]{0,1:T(8,128)(2,1)S(1)}, u32[]{:S(2)}) copy-start(bf16[128,384]{0,1:T(8,128)(2,1)S(1)} %fusion.30) | copy-start | bytes 294916
  594.3 3.2 collective-permute-start.6
  641.1 46.1 %copy-start.1 = (f32[1,24,32,512]{3,2,1,0:T(8,128)S(1)}, f32[1,24,32,512]{3,2,1,0:T(8,128)}, u32[]{:S(2)}) copy-start(f32[1,24,32,512]{3,2,1,0:T(8,128)} %param.11) | copy-start | bytes 4718596
  694.7 27.7 %all-to-all-start = ((bf16[16,3,32,512]{3,2,1,0:T(8,128)(2,1)}), bf16[16,3,32,512]{3,2,1,0:T(8,128)(2,1)S(1)}, u32[]{:S(2)}, u32[]{:S(2)}) async-start(bf16[16,3,32,512]{3,2,1,0:T(8,128)(2,1)} %convert_element_type.176), calls=%async_computation | async-start | bytes 3145728 | tf_op jit(solution)/shard_map/all_to_all | solution.py:74
  699.7 84.4 %reduce-scatter.39.cloned.1.call-start = ((), (), s32[]{:S(2)}) async-start(), calls=%async_computation.19 | async-start | bytes 1671168
  708.6 14.3 %copy-start = (f32[16,32,512]{2,1,0:T(8,128)S(1)}, f32[16,32,512]{2,1,0:T(8,128)}, u32[]{:S(2)}) copy-start(f32[16,32,512]{2,1,0:T(8,128)} %fusion.19) | copy-start | bytes 3145732
  708.6 138.3 %all-gather.7.cloned.1.call-start = ((), (), s32[]{:S(2)}) async-start(), calls=%async_computation.10 | async-start | bytes 6684672 | tf_op jit(solution)/shard_map/all_gather | solution.py:110
  735.6 48.5 %copy-start.5 = (bf16[128,384]{0,1:T(8,128)(2,1)S(1)}, bf16[128,384]{0,1:T(8,128)(2,1)}, u32[]{:S(2)}) copy-start(bf16[128,384]{0,1:T(8,128)(2,1)} %copy-done.4) | copy-start | bytes 294916
  735.6 48.5 %copy-start.7 = (bf16[128,384]{0,1:T(8,128)(2,1)S(1)}, bf16[128,384]{0,1:T(8,128)(2,1)}, u32[]{:S(2)}) copy-start(bf16[128,384]{0,1:T(8,128)(2,1)} %copy-done.6) | copy-start | bytes 294916
  735.6 48.5 %copy-start.9 = (bf16[128,384]{0,1:T(8,128)(2,1)S(1)}, bf16[128,384]{0,1:T(8,128)(2,1)}, u32[]{:S(2)}) copy-start(bf16[128,384]{0,1:T(8,128)(2,1)} %copy-done.8) | copy-start | bytes 294916
  735.6 48.4 %copy-start.11 = (bf16[128,384]{0,1:T(8,128)(2,1)S(1)}, bf16[128,384]{0,1:T(8,128)(2,1)}, u32[]{:S(2)}) copy-start(bf16[128,384]{0,1:T(8,128)(2,1)} %copy-done.10) | copy-start | bytes 294916
  735.6 48.4 %copy-start.13 = (bf16[128,384]{0,1:T(8,128)(2,1)S(1)}, bf16[128,384]{0,1:T(8,128)(2,1)}, u32[]{:S(2)}) copy-start(bf16[128,384]{0,1:T(8,128)(2,1)} %copy-done.12) | copy-start | bytes 294916
  (7 other events, 21.5 us)
Sparse Core Ops, SparseCore 0:
  12.3 76.3 reduce-scatter.24
  97.9 74.8 reduce-scatter.26
  181.9 74.8 reduce-scatter.28
  266.1 74.8 reduce-scatter.30
  350.2 74.9 reduce-scatter.32
  434.4 74.8 reduce-scatter.34
  518.5 74.9 reduce-scatter.36
  595.6 43.2 all-gather.8
  641.7 43.3 all-gather.4
  708.7 75.3 reduce-scatter.38
  786.2 60.6 all-gather.6
where the time goes:
time: 865 us; the launch traced here: 863 us
  waiting for transfers between devices  735 us (85%)
  matrix products  43.6 us (5%)
  local copies, waits for them, and re-layouts  31.8 us (4%)
  other arithmetic  19.5 us (2%)
  between operations  18.3 us (2%)
  starting transfers between devices  14.6 us (2%)
    unnamed x19, waiting for transfers between devices  569 us
    all_gather x1, waiting for transfers between devices, shards(): gathered = lax.all_gather(stacked, 'dp', axis=0, tiled=True)  59.8 us
    all_gather x1, waiting for transfers between devices, shards(): lax.all_gather(out_grads, 'dp', axis=1, tiled=True)  44 us
    all_gather x1, waiting for transfers between devices, shards(): lax.all_gather(acts_local, 'dp', axis=1, tiled=True)  35.1 us
    dot_general x8, matrix products, shards(): jnp.dot(incoming, weight_rows, preferred_element_type=jnp.float32)  26.8 us
  transfers between devices with their start and end apart: 19, of which 19 were waited for; matrix products, arithmetic and copies ran while one was open for 4% of the time, Pallas kernels for 0%

commit v1 on v0

v1 whole, which is shorter than its diff:
```python
import jax
import jax.numpy as jnp
from jax import lax
from jax.experimental import pallas as pl
from jax.experimental.pallas import tpu as pltpu
from jax.sharding import PartitionSpec as P

BLOCK = 512
ROWS = 128
MOST = 3
NBLK = 12
TILES = 24
N_DP = 16
SIDE = 4
SECTIONS = 8
WIDTH = 384
CHUNK = 128
PER = WIDTH // CHUNK
GRADS = NBLK * BLOCK // CHUNK
SLICE = BLOCK // N_DP
STRIPE = 64
DECAY = 0.8
DAMP = 0.1
MESH = pl.DeviceIdType.MESH


def kernel(
    table, counts, acts, grad_top, slopes, weights, running,
    backs_o, pre_acts_o, pre_grads_o, inverses_o,
    w_s, run_s, rows_s, outbox, held, xall, inc, parts, terms, acc,
    mat_a, mat_b, fb, xb, rem, inv, pre,
    load_sem, hop_send, hop_recv,
    rs_send, rs_recv, ag_send, ag_recv, ax_send, ax_recv,
    ra_send, ra_recv, rb_send, rb_recv, rc_send, rc_recv,
):
    me = lax.axis_index("dp")
    sec = lax.axis_index("section")
    my_x, my_z = me // SIDE, me % SIDE

    def to(r):
        return ((my_x + r // SIDE) % SIDE) * SIDE + (my_z + r % SIDE) % SIDE

    def source(r):
        return ((my_x + SIDE - r // SIDE) % SIDE) * SIDE + (my_z + SIDE - r % SIDE) % SIDE

    def base_of(d):
        return 3 * (d // 4) + (d % 4) // 2

    w_copy = pltpu.make_async_copy(weights, w_s, load_sem.at[0])
    run_copy = pltpu.make_async_copy(running, run_s, load_sem.at[1])
    w_copy.start()
    run_copy.start()

    barrier = pltpu.get_barrier_semaphore()

    @pl.loop(1, N_DP)
    def _(r):
        pl.semaphore_signal(barrier, inc=1, device_id=(to(r), sec), device_id_type=MESH)

    @pl.when(sec > 0)
    def _():
        pl.semaphore_signal(barrier, inc=1, device_id=(me, sec - 1), device_id_type=MESH)

    @pl.when(sec < SECTIONS - 1)
    def _():
        pl.semaphore_signal(barrier, inc=1, device_id=(me, sec + 1), device_id_type=MESH)

    edge = jnp.where((sec == 0) | (sec == SECTIONS - 1), 1, 0)
    pl.semaphore_wait(barrier, N_DP + 1 - edge)

    def rs_copy(r):
        return pltpu.make_async_remote_copy(
            parts.at[r], terms.at[r], rs_send.at[r], rs_recv.at[r],
            device_id=(to(r), sec), device_id_type=MESH)

    def gather_copy(r, first, send, recv, peer, owner):
        mine = xall.at[pl.ds(first + PER * owner, PER)]
        return pltpu.make_async_remote_copy(
            mine, mine, send.at[r], recv.at[r], device_id=(peer, sec), device_id_type=MESH)

    def ax_copy(r, owner):
        return gather_copy(r, 0, ax_send, ax_recv, to(r), owner)

    def ag_copy(r, owner):
        return gather_copy(r, GRADS, ag_send, ag_recv, to(r), owner)

    def ra_copy(r, owner):
        peer = to(r)
        return pltpu.make_async_remote_copy(
            outbox.at[pl.ds(MOST * peer, MOST)],
            held.at[pl.ds(4, MOST), pl.ds(pl.multiple_of(SLICE * owner, SLICE), SLICE)],
            ra_send.at[r], ra_recv.at[r], device_id=(peer, sec), device_id_type=MESH)

    def rb_copy(r, owner):
        peer = to(r)
        return pltpu.make_async_remote_copy(
            rows_s.at[pl.ds(base_of(peer), 2)],
            held.at[pl.ds(0, 2), pl.ds(pl.multiple_of(SLICE * owner, SLICE), SLICE)],
            rb_send.at[r], rb_recv.at[r], device_id=(peer, sec), device_id_type=MESH)

    def rc_copy(r, owner):
        peer = to(r)
        return pltpu.make_async_remote_copy(
            rows_s.at[pl.ds(NBLK + base_of(peer), 2)],
            held.at[pl.ds(2, 2), pl.ds(pl.multiple_of(SLICE * owner, SLICE), SLICE)],
            rc_send.at[r], rc_recv.at[r], device_id=(peer, sec), device_id_type=MESH)

    def redistribute():
        run_copy.wait()
        for i in range(PER):
            xall[PER * me + i] = acts[:, i * CHUNK:(i + 1) * CHUNK]

        @pl.loop(1, N_DP)
        def _(r):
            ax_copy(r, me).start()

        @pl.loop(0, TILES)
        def _(t):
            rows_s[t] = run_s[t].astype(jnp.bfloat16)

        @pl.loop(1, N_DP)
        def _(r):
            rb_copy(r, me).start()
            rc_copy(r, me).start()

        @pl.loop(0, N_DP * MOST)
        def _(q):
            outbox[q] = rows_s[jnp.maximum(table[q], 0)]

        @pl.loop(1, N_DP)
        def _(r):
            ra_copy(r, me).start()

        own = pl.ds(pl.multiple_of(SLICE * me, SLICE), SLICE)
        for k in range(2):
            held[k, own] = rows_s[base_of(me) + k]
            held[2 + k, own] = rows_s[NBLK + base_of(me) + k]
        for m in range(MOST):
            held[4 + m, own] = outbox[MOST * me + m]

    pl.when(sec < SECTIONS // 2)(redistribute)

    hop = pltpu.make_async_remote_copy(
        backs_o, inc, hop_send, hop_recv, device_id=(me, jnp.maximum(sec - 1, 0)), device_id_type=MESH)

    @pl.when(sec == SECTIONS - 1)
    def _():
        inc[...] = grad_top[...]

    @pl.when(sec < SECTIONS - 1)
    def _():
        hop.wait_recv()

    for i in range(PER):
        xall[GRADS + PER * me + i] = inc[:, i * CHUNK:(i + 1) * CHUNK]

    def gather_grads():
        @pl.loop(1, N_DP)
        def _(r):
            ag_copy(r, me).start()

    pl.when(sec == 0)(gather_grads)
    w_copy.wait()

    def part(r):
        columns = pl.ds(pl.multiple_of(WIDTH * to(r), CHUNK), WIDTH)
        return jnp.dot(inc[...], w_s[:, columns], preferred_element_type=jnp.float32).astype(jnp.bfloat16)

    @pl.loop(1, N_DP)
    def _(r):
        parts[r] = part(r)
        rs_copy(r).start()

    acc[...] = part(0).astype(jnp.float32)
    pl.when(sec > 0)(gather_grads)

    @pl.loop(1, N_DP)
    def _(r):
        rs_copy(r).wait_recv()
        acc[...] += terms[r].astype(jnp.float32)

    backs_o[...] = (acc[...] * slopes[...].astype(jnp.float32)).astype(jnp.bfloat16)

    @pl.when(sec > 0)
    def _():
        hop.start()

    pl.when(sec >= SECTIONS // 2)(redistribute)

    def diagonal(at):
        row = lax.broadcasted_iota(jnp.int32, (STRIPE, BLOCK), 0) + at * STRIPE
        return row == lax.broadcasted_iota(jnp.int32, (STRIPE, BLOCK), 1)

    def tile(i, owned):
        if owned:
            entry = table[MOST * me + i - 4]
            which = jnp.maximum(entry, 0)
        else:
            which = base_of(me) + jnp.where(i < 2, i, NBLK - 2 + i)
        x = jnp.concatenate([xall[4 * which + k] for k in range(4)], axis=1)
        mat_a[...] = lax.dot_general(x, x, (((0,), (0,)), ((), ())), preferred_element_type=jnp.float32)
        total = jnp.zeros((8, BLOCK), jnp.float32)
        for at in range(BLOCK // STRIPE):
            rows = pl.ds(at * STRIPE, STRIPE)
            value = DECAY * held[i, rows].astype(jnp.float32) + ((1.0 - DECAY) / ROWS) * mat_a[rows]
            value = value + jnp.where(diagonal(at), DAMP, 0.0)
            mat_a[rows] = value
            fb[rows] = value.astype(jnp.bfloat16)
            total = total + jnp.sum(jnp.abs(value).reshape(STRIPE // 8, 8, BLOCK), axis=0)
        scale = jnp.max(jnp.sum(total, axis=0, keepdims=True), axis=1, keepdims=True)
        recip = 1.0 / scale
        for at in range(BLOCK // STRIPE):
            rows = pl.ds(at * STRIPE, STRIPE)
            xb[rows] = ((jnp.where(diagonal(at), 2.0, 0.0) - mat_a[rows] * recip) * recip).astype(jnp.bfloat16)
        mat_b[...] = jnp.dot(fb[...], xb[...], preferred_element_type=jnp.float32)
        for at in range(BLOCK // STRIPE):
            rows = pl.ds(at * STRIPE, STRIPE)
            rem[rows] = (jnp.where(diagonal(at), 2.0, 0.0) - mat_b[rows]).astype(jnp.bfloat16)
        mat_b[...] = jnp.dot(xb[...], rem[...], preferred_element_type=jnp.float32)
        twice = counts[which] > 1
        for at in range(BLOCK // STRIPE):
            rows = pl.ds(at * STRIPE, STRIPE)
            inv[rows] = jnp.where(twice, mat_b[rows], xb[rows].astype(jnp.float32)).astype(jnp.bfloat16)

        if owned:
            inverses_o[i - 4] = jnp.where(entry >= 0, inv[...].astype(jnp.float32), 0.0).astype(jnp.bfloat16)
        else:
            pre[i] = jnp.dot(x, inv[...], preferred_element_type=jnp.float32).astype(jnp.bfloat16)

    def columns_out(out, first):
        start = 3 * me - 4 * base_of(me)
        for i in range(PER):
            at = start + i
            lane = pl.ds(pl.multiple_of((at % 4) * CHUNK, CHUNK), CHUNK)
            out[:, i * CHUNK:(i + 1) * CHUNK] = pre[first + at // 4, :, lane]

    @pl.loop(1, N_DP)
    def _(r):
        ax_copy(r, source(r)).wait_recv()
        rb_copy(r, source(r)).wait_recv()

    @pl.loop(0, 2)
    def _(i):
        tile(i, False)

    columns_out(pre_acts_o, 0)

    @pl.loop(1, N_DP)
    def _(r):
        ag_copy(r, source(r)).wait_recv()
        rc_copy(r, source(r)).wait_recv()
        ra_copy(r, source(r)).wait_recv()

    @pl.loop(2, 4)
    def _(i):
        tile(i, False)

    columns_out(pre_grads_o, 2)

    @pl.loop(4, 4 + MOST)
    def _(i):
        tile(i, True)

    @pl.loop(1, N_DP)
    def _(r):
        rs_copy(r).wait_send()
        ax_copy(r, me).wait_send()
        ag_copy(r, me).wait_send()
        ra_copy(r, me).wait_send()
        rb_copy(r, me).wait_send()
        rc_copy(r, me).wait_send()

    @pl.when(sec > 0)
    def _():
        hop.wait_send()


def shards(acts, grad_top, weights_t, slopes, running, ns_counts, assignment):
    owners = assignment[0]
    tile_ids = jnp.arange(TILES, dtype=jnp.int32)
    matches = (owners[:, None] == owners[None, :]) & (tile_ids[None, :] < tile_ids[:, None])
    slots_of = jnp.sum(matches.astype(jnp.int32), axis=1)
    places = jnp.arange(N_DP * MOST, dtype=jnp.int32)
    taken = (owners * MOST + slots_of)[None, :] == places[:, None]
    table = jnp.sum(jnp.where(taken, tile_ids[None, :] + 1, 0), axis=1) - 1
    vmem = pl.BlockSpec(memory_space=pltpu.VMEM)
    smem = pl.BlockSpec(memory_space=pltpu.SMEM)
    hbm = pl.BlockSpec(memory_space=pl.ANY)
    bf16, f32 = jnp.bfloat16, jnp.float32
    flat = jax.ShapeDtypeStruct((ROWS, WIDTH), bf16)
    dma = pltpu.SemaphoreType.DMA
    backs, pre_acts, pre_grads, inverses = pl.pallas_call(
        kernel,
        out_shape=(flat, flat, flat, jax.ShapeDtypeStruct((MOST, BLOCK, BLOCK), bf16)),
        in_specs=[smem, smem, vmem, vmem, vmem, hbm, hbm],
        out_specs=(vmem, vmem, vmem, vmem),
        scratch_shapes=[
            pltpu.VMEM((WIDTH, NBLK * BLOCK), bf16),
            pltpu.VMEM((TILES, SLICE, BLOCK), f32),
            pltpu.VMEM((TILES, SLICE, BLOCK), bf16),
            pltpu.VMEM((N_DP * MOST, SLICE, BLOCK), bf16),
            pltpu.VMEM((4 + MOST, BLOCK, BLOCK), bf16),
            pltpu.VMEM((2 * GRADS, ROWS, CHUNK), bf16),
            pltpu.VMEM((ROWS, WIDTH), bf16),
            pltpu.VMEM((N_DP, ROWS, WIDTH), bf16),
            pltpu.VMEM((N_DP, ROWS, WIDTH), bf16),
            pltpu.VMEM((ROWS, WIDTH), f32),
            pltpu.VMEM((BLOCK, BLOCK), f32),
            pltpu.VMEM((BLOCK, BLOCK), f32),
            pltpu.VMEM((BLOCK, BLOCK), bf16),
            pltpu.VMEM((BLOCK, BLOCK), bf16),
            pltpu.VMEM((BLOCK, BLOCK), bf16),
            pltpu.VMEM((BLOCK, BLOCK), bf16),
            pltpu.VMEM((4, ROWS, BLOCK), bf16),
            dma((2,)), dma, dma,
        ] + [dma((N_DP,))] * 12,
        compiler_params=pltpu.CompilerParams(
            collective_id=0, has_side_effects=True, vmem_limit_bytes=48 * 1024 * 1024),
        name="refresh",
    )(table, ns_counts[0], acts[0], grad_top, slopes[0], weights_t[0], running[0])
    return (backs[None], pre_acts[None], pre_grads[None], inverses[None, None])


def solution(mesh):
    in_specs = (
        P("section", None, "dp"),
        P(None, "dp"),
        P("section", "dp", None),
        P("section", None, "dp"),
        P("section", None, "dp", None),
        P("section", None),
        P("section", None),
    )
    out_specs = (
        P("section", None, "dp"),
        P("section", None, "dp"),
        P("section", None, "dp"),
        P("section", "dp", None, None, None),
    )
    return jax.shard_map(shards, mesh=mesh, in_specs=in_specs, out_specs=out_specs, check_vma=False)
```

time: 865 us -> 208 us (0.24)
  waiting for transfers between devices: 735 us -> 0 us
  Pallas kernels: 0 us -> 198 us
  matrix products: 43.6 us -> 0 us
  local copies, waits for them, and re-layouts: 31.8 us -> 7.8 us
  other arithmetic: 19.5 us -> 1.67 us
  between operations: 18.3 us -> 0.65 us
  starting transfers between devices: 14.6 us -> 0 us
    unnamed x19 -> x0, waiting for transfers between devices: 569 us -> none
    pallas_call x0 -> x1, Pallas kernels: none -> 198 us  [shards(): pl.pallas_call(kernel, out_shape=(flat, flat, flat, jax.ShapeDtypeStruct(...]
    all_gather x3 -> x0, waiting for transfers between devices: 139 us -> none  [the longest x1 59.8 us: shards(): gathered = lax.all_gather(stacked, 'dp', axis=0, tiled=True)]
    dot_general x14 -> x0, matrix products: 43.6 us -> none  [the longest x8 26.8 us: shards(): jnp.dot(incoming, weight_rows, preferred_element_type=jnp.float32)]
    all_to_all x1 -> x0, waiting for transfers between devices: 13.8 us -> none  [shards(): lax.all_to_all(outbox.astype(jnp.bfloat16), 'dp', split_axis=0, concat_ax...]
    ppermute x7 -> x0, waiting for transfers between devices: 12.9 us -> none  [from_behind(): return lax.ppermute(block, axis, route)]
    convert_element_type x11 -> x0, other arithmetic: 10.6 us -> none  [the longest x7 6.44 us: shards(): backward = (summed * slope_local).astype(jnp.bfloat16)]
    ppermute x7 -> x0, starting transfers between devices: 9.23 us -> none  [from_behind(): return lax.ppermute(block, axis, route)]
  transfers between devices with their start and end apart: 19 -> 0, of which waited for: 19 -> 0; matrix products, arithmetic and copies ran while one was open for 4% -> 0% of each run, Pallas kernels for 0% -> 0%
where the time goes in v1:
time: 208 us
  Pallas kernels  198 us (95%)
  local copies, waits for them, and re-layouts  7.8 us (4%)
    pallas_call x1, Pallas kernels, shards(): pl.pallas_call(kernel, out_shape=(flat, flat, flat, jax.ShapeDtypeStruct(...  198 us
    unnamed x14, local copies, waits for them, and re-layouts  7.8 us

profile of v1, /device:TPU:0, one launch (start us, length us, event | category | flops | bytes accessed | tf_op | source)
XLA Modules:
  0.0 208.2 jit_solution(5870244106396799387)
XLA Ops:
  0.6 0.9 convert_reduce_fusion
  1.5 0.7 fusion.1
  2.2 0.1 select_reduce_fusion
  2.3 0.0 copy-start
  2.3 1.4 copy-done
  3.7 0.0 copy-start.1
  3.7 0.9 copy-done.1
  4.6 0.0 copy-start.2
  4.6 0.9 copy-done.2
  5.5 0.0 copy-start.3
  5.5 0.9 copy-done.3
  6.4 0.0 copy-start.4
  6.4 0.7 copy-done.4
  7.1 198.1 %refresh.1 = (bf16[128,384]{1,0:T(8,128)(2,1)S(1)}, bf16[128,384]{1,0:T(8,128)(2,1)S(1)}, bf16[128,384]{1,0:T(8,128)(2,1)S(1)}, bf16[3,512,512]{2,1,0:T(8,128)(2,1)S(1)}) custom-call(s32[48]{0:T(128)S(1)} %broadcast_add_fusion.table, s32[24]{0:T(128)S(1)} %bitcast.23, bf16[128,384]{1,0:T(8,128)(2,1)S(1)} %bitcast.21, bf16[128,384]{1,0:T(8,128)(2,1)S(1)} %copy-done.2, ...), custom_call_target="tpu_custom_call" | custom-call | tf_op jit(solution)/shard_map/refresh/pallas_call | solution.py:292
  205.1 0.6 copy.15
  205.8 0.6 copy.16
  206.4 0.6 copy.17
  207.0 1.1 copy.18
  (2 shorter events, 0.0 us)
Async XLA Ops:
  2.3 1.4 copy-start
  3.7 0.9 copy-start.1
  4.6 0.9 copy-start.2
  5.5 0.9 copy-start.3
  6.4 0.7 copy-start.4

commit v2 on v1

v2 whole, which is shorter than its diff:
```python
import jax
import jax.numpy as jnp
from jax import lax
from jax.experimental import pallas as pl
from jax.experimental.pallas import tpu as pltpu
from jax.sharding import PartitionSpec as P

BLOCK = 512
ROWS = 128
MOST = 3
NBLK = 12
TILES = 24
N_DP = 16
SIDE = 4
SECTIONS = 8
WIDTH = 384
CHUNK = 128
PER = WIDTH // CHUNK
CHUNKS = 2 * NBLK * BLOCK // CHUNK
SLICE = BLOCK // N_DP
GROUP = 16
PLACES = N_DP * MOST
STRIPE = 64
PARTS = 4
LOT = ROWS // PARTS
DECAY = 0.8
DAMP = 0.1
MESH = pl.DeviceIdType.MESH
BF16 = jnp.bfloat16
F32 = jnp.float32


def far_first(k):
    return jnp.where(k == 0, 2, jnp.where(k == 1, 1, jnp.where(k == 2, 3, 0)))


def kernel(
    table, place, counts, acts, grad_top, slopes, weights, running,
    backs_o, pre_acts_o, pre_grads_o, inverses_o,
    w_s, run_s, acts_s, slopes_s, rows_s, outbox, held,
    inc, parts, terms, own_x, xrow, fbox, xs, pbox, prcv, prow, pin,
    mat_a, mat_b, fb, xb, rem, inv,
    w_sem, load_sem, hop_send, hop_recv, rs_send, rs_recv, pause,
    ra_send, ra_recv, fa_send, fa_recv, fg_send, fg_recv,
    f2_send, f2_recv, b1_send, b1_recv, b2_send, b2_recv,
):
    me = lax.axis_index("dp")
    sec = lax.axis_index("section")
    my_x, my_z = me // SIDE, me % SIDE
    my_group, my_half = me // 2, me % 2

    def to(r):
        return ((my_x + r // SIDE) % SIDE) * SIDE + (my_z + r % SIDE) % SIDE

    def source(r):
        return ((my_x + SIDE - r // SIDE) % SIDE) * SIDE + (my_z + SIDE - r % SIDE) % SIDE

    def remote(src, dst, send, recv, peer):
        return pltpu.make_async_remote_copy(
            src, dst, send, recv, device_id=(peer, sec), device_id_type=MESH)

    def each_peer(body):
        @pl.loop(0, N_DP - 1)
        def _(k):
            body(far_first(k // SIDE) * SIDE + far_first(k % SIDE))

    def w_copy(x):
        columns = pl.ds(pl.multiple_of(x * (SIDE * WIDTH), CHUNK), SIDE * WIDTH)
        return pltpu.make_async_copy(weights.at[:, columns], w_s.at[:, columns], w_sem.at[x])

    run_copy = pltpu.make_async_copy(running, run_s, load_sem.at[0])
    acts_copy = pltpu.make_async_copy(acts, acts_s, load_sem.at[1])
    slopes_copy = pltpu.make_async_copy(slopes, slopes_s, load_sem.at[2])
    top_copy = pltpu.make_async_copy(grad_top, inc, load_sem.at[3])

    @pl.when(sec == SECTIONS - 1)
    def _():
        top_copy.start()

    for k in (2, 1, 3, 0):
        w_copy((my_x + k) % SIDE).start()
    slopes_copy.start()
    acts_copy.start()
    run_copy.start()

    barrier = pltpu.get_barrier_semaphore()
    each_peer(lambda r: pl.semaphore_signal(barrier, inc=1, device_id=(to(r), sec), device_id_type=MESH))

    @pl.when(sec > 0)
    def _():
        pl.semaphore_signal(barrier, inc=1, device_id=(me, sec - 1), device_id_type=MESH)

    @pl.when(sec < SECTIONS - 1)
    def _():
        pl.semaphore_signal(barrier, inc=1, device_id=(me, sec + 1), device_id_type=MESH)

    edge = jnp.where((sec == 0) | (sec == SECTIONS - 1), 1, 0)
    pl.semaphore_wait(barrier, N_DP + 1 - edge)

    def group_rows(d):
        return pl.ds(pl.multiple_of(GROUP * (d // 2), GROUP), GROUP)

    def ra_copy(r, owner):
        return remote(
            outbox.at[pl.ds(MOST * to(r), MOST)],
            held.at[:, pl.ds(pl.multiple_of(SLICE * owner, SLICE), SLICE)],
            ra_send.at[r], ra_recv.at[r], to(r))

    def fa_copy(r, owner):
        return remote(
            own_x.at[pl.ds(0, PER), group_rows(to(r))], xrow.at[pl.ds(PER * owner, PER)],
            fa_send.at[r], fa_recv.at[r], to(r))

    def fg_copy(r, owner):
        return remote(
            own_x.at[pl.ds(PER, PER), group_rows(to(r))], xrow.at[pl.ds(CHUNKS // 2 + PER * owner, PER)],
            fg_send.at[r], fg_recv.at[r], to(r))

    def f2_copy(r, owner):
        return remote(
            fbox.at[pl.ds(MOST * to(r), MOST)], xs.at[:, owner % 2, :, group_rows(owner)],
            f2_send.at[r], f2_recv.at[r], to(r))

    def b1_copy(r, owner):
        peer = to(r)
        return remote(
            pbox.at[:, peer % 2, :, group_rows(peer)], prcv.at[pl.ds(MOST * owner, MOST)],
            b1_send.at[r], b1_recv.at[r], peer)

    def pair_of(f, half):
        k = f % 4
        return 3 * (f // 4) + jnp.where(k == 0, 0, jnp.where(k == 3, 2, k - half))

    def b2_copy(r, owner):
        return remote(
            prow.at[pair_of(to(r), my_half)], pin.at[owner % 2, :, :, group_rows(owner)],
            b2_send.at[r], b2_recv.at[r], to(r))

    def prepare():
        acts_copy.wait()
        for i in range(PER):
            own_x[i] = acts_s[:, i * CHUNK:(i + 1) * CHUNK]
        each_peer(lambda r: fa_copy(r, me).start())
        xrow[pl.ds(PER * me, PER)] = own_x[pl.ds(0, PER), group_rows(me)]
        run_copy.wait()

        @pl.loop(0, TILES)
        def _(t):
            rows_s[t] = run_s[t].astype(BF16)

        @pl.loop(0, PLACES)
        def _(q):
            outbox[q] = rows_s[jnp.maximum(table[q], 0)]

        each_peer(lambda r: ra_copy(r, me).start())
        held[:, pl.ds(pl.multiple_of(SLICE * me, SLICE), SLICE)] = outbox[pl.ds(MOST * me, MOST)]

    pl.when(sec < SECTIONS - 2)(prepare)

    @pl.when(sec == SECTIONS - 1)
    def _():
        top_copy.wait()

    def lot(m):
        return pl.ds(pl.multiple_of(LOT * m, LOT), LOT)

    def hop(m):
        return pltpu.make_async_remote_copy(
            backs_o.at[lot(m)], inc.at[lot(m)], hop_send.at[m], hop_recv.at[m],
            device_id=(me, jnp.maximum(sec - 1, 0)), device_id_type=MESH)

    def rs_copy(m, r):
        return remote(parts.at[m, to(r)], terms.at[m, r], rs_send.at[m, r], rs_recv.at[m, r], to(r))

    def spread_grads():
        for i in range(PER):
            own_x[PER + i] = inc[:, i * CHUNK:(i + 1) * CHUNK]
        each_peer(lambda r: fg_copy(r, me).start())
        xrow[pl.ds(CHUNKS // 2 + PER * me, PER)] = own_x[pl.ds(PER, PER), group_rows(me)]

    @pl.loop(0, PARTS)
    def _(m):
        @pl.when(sec < SECTIONS - 1)
        def _():
            hop(m).wait_recv()

        pl.when((sec < 2) & (m == PARTS - 1))(spread_grads)

        @pl.loop(0, SIDE)
        def _(a):
            x = (my_x + far_first(a)) % SIDE

            @pl.when(m == 0)
            def _():
                w_copy(x).wait()

            columns = pl.ds(pl.multiple_of(x * (SIDE * WIDTH), CHUNK), SIDE * WIDTH)
            product = jnp.dot(inc[lot(m)], w_s[:, columns], preferred_element_type=F32).astype(BF16)
            for z in range(SIDE):
                parts[m, x * SIDE + z] = product[:, z * WIDTH:(z + 1) * WIDTH]

            @pl.loop(0, SIDE)
            def _(b):
                r = far_first(a) * SIDE + far_first(b)

                @pl.when(r > 0)
                def _():
                    rs_copy(m, r).start()

    slopes_copy.wait()

    @pl.loop(0, PARTS)
    def _(m):
        def add(k, total):
            r = far_first(3 - k // SIDE) * SIDE + far_first(3 - k % SIDE)
            rs_copy(m, r).wait_recv()
            return total + terms[m, r].astype(F32)

        total = lax.fori_loop(1, N_DP, add, parts[m, me].astype(F32))
        backs_o[lot(m)] = (total * slopes_s[lot(m)].astype(F32)).astype(BF16)

        @pl.when(sec > 0)
        def _():
            hop(m).start()

    even = sec % 2 == 0

    @pl.when(even & (sec > 0))
    def _():
        pl.semaphore_signal(pause, inc=1, device_id=(me, sec + 1), device_id_type=MESH)

    @pl.when(jnp.logical_not(even) & (sec > 1))
    def _():
        pl.semaphore_wait(pause, 1)

    pl.when(sec >= SECTIONS - 2)(prepare)
    pl.when(sec >= 2)(spread_grads)

    @pl.loop(1, N_DP)
    def _(r):
        fa_copy(r, source(r)).wait_recv()
        fg_copy(r, source(r)).wait_recv()

    @pl.loop(0, PLACES)
    def _(q):
        first = 4 * jnp.maximum(table[q], 0) + 2 * my_half
        fbox[q, 0] = xrow[first]
        fbox[q, 1] = xrow[first + 1]

    each_peer(lambda r: f2_copy(r, me).start())
    for m in range(MOST):
        xs[m, my_half, :, group_rows(me)] = fbox[MOST * me + m]

    @pl.loop(1, N_DP)
    def _(r):
        ra_copy(r, source(r)).wait_recv()
        f2_copy(r, source(r)).wait_recv()

    def diagonal(at):
        row = lax.broadcasted_iota(jnp.int32, (STRIPE, BLOCK), 0) + at * STRIPE
        return row == lax.broadcasted_iota(jnp.int32, (STRIPE, BLOCK), 1)

    @pl.loop(0, MOST)
    def _(m):
        entry = table[MOST * me + m]
        twice = counts[jnp.maximum(entry, 0)] > 1
        x = jnp.concatenate([xs[m, k // 2, k % 2] for k in range(4)], axis=1)
        mat_a[...] = lax.dot_general(x, x, (((0,), (0,)), ((), ())), preferred_element_type=F32)
        total = jnp.zeros((8, BLOCK), F32)
        for at in range(BLOCK // STRIPE):
            rows = pl.ds(at * STRIPE, STRIPE)
            value = DECAY * held[m, rows].astype(F32) + ((1.0 - DECAY) / ROWS) * mat_a[rows]
            value = value + jnp.where(diagonal(at), DAMP, 0.0)
            mat_a[rows] = value
            fb[rows] = value.astype(BF16)
            total = total + jnp.sum(jnp.abs(value).reshape(STRIPE // 8, 8, BLOCK), axis=0)
        scale = jnp.max(jnp.sum(total, axis=0, keepdims=True), axis=1, keepdims=True)
        recip = 1.0 / scale
        for at in range(BLOCK // STRIPE):
            rows = pl.ds(at * STRIPE, STRIPE)
            xb[rows] = ((jnp.where(diagonal(at), 2.0, 0.0) - mat_a[rows] * recip) * recip).astype(BF16)
        mat_b[...] = jnp.dot(fb[...], xb[...], preferred_element_type=F32)
        for at in range(BLOCK // STRIPE):
            rows = pl.ds(at * STRIPE, STRIPE)
            rem[rows] = (jnp.where(diagonal(at), 2.0, 0.0) - mat_b[rows]).astype(BF16)
        mat_b[...] = jnp.dot(xb[...], rem[...], preferred_element_type=F32)
        for at in range(BLOCK // STRIPE):
            rows = pl.ds(at * STRIPE, STRIPE)
            chosen = jnp.where(twice, mat_b[rows], xb[rows].astype(F32))
            inv[rows] = chosen.astype(BF16)
            inverses_o[m, rows] = jnp.where(entry >= 0, chosen, 0.0).astype(BF16)
        result = jnp.dot(x, inv[...], preferred_element_type=F32).astype(BF16)
        for k in range(4):
            pbox[m, k // 2, k % 2] = result[:, k * CHUNK:(k + 1) * CHUNK]

    each_peer(lambda r: b1_copy(r, me).start())
    for m in range(MOST):
        prcv[MOST * me + m] = pbox[m, my_half, :, group_rows(me)]

    @pl.loop(1, N_DP)
    def _(r):
        b1_copy(r, source(r)).wait_recv()

    for t in range(TILES):
        prow[t % NBLK, t // NBLK] = prcv[place[t]]

    each_peer(lambda r: b2_copy(r, me).start())
    pin[my_half, :, :, group_rows(me)] = prow[pair_of(me, my_half)]

    @pl.loop(1, N_DP)
    def _(r):
        b2_copy(r, source(r)).wait_recv()

    for i in range(PER):
        c = PER * me + i
        lanes = slice(i * CHUNK, (i + 1) * CHUNK)
        pre_acts_o[:, lanes] = pin[(c % 4) // 2, 0, c % 2]
        pre_grads_o[:, lanes] = pin[(c % 4) // 2, 1, c % 2]

    @pl.loop(1, N_DP)
    def _(r):
        ra_copy(r, me).wait_send()
        fa_copy(r, me).wait_send()
        fg_copy(r, me).wait_send()
        f2_copy(r, me).wait_send()
        b1_copy(r, me).wait_send()
        b2_copy(r, me).wait_send()

        @pl.loop(0, PARTS)
        def _(m):
            rs_copy(m, r).wait_send()

    @pl.when(sec > 0)
    def _():
        @pl.loop(0, PARTS)
        def _(m):
            hop(m).wait_send()


def shards(acts, grad_top, weights_t, slopes, running, ns_counts, assignment):
    owners = assignment[0]
    tile_ids = jnp.arange(TILES, dtype=jnp.int32)
    matches = (owners[:, None] == owners[None, :]) & (tile_ids[None, :] < tile_ids[:, None])
    place = owners * MOST + jnp.sum(matches.astype(jnp.int32), axis=1)
    taken = place[None, :] == jnp.arange(PLACES, dtype=jnp.int32)[:, None]
    table = jnp.sum(jnp.where(taken, tile_ids[None, :] + 1, 0), axis=1) - 1
    vmem = pl.BlockSpec(memory_space=pltpu.VMEM)
    smem = pl.BlockSpec(memory_space=pltpu.SMEM)
    hbm = pl.BlockSpec(memory_space=pl.ANY)
    flat = jax.ShapeDtypeStruct((ROWS, WIDTH), BF16)
    dma = pltpu.SemaphoreType.DMA
    square = (BLOCK, BLOCK)
    backs, pre_acts, pre_grads, inverses = pl.pallas_call(
        kernel,
        out_shape=(flat, flat, flat, jax.ShapeDtypeStruct((MOST,) + square, BF16)),
        in_specs=[smem, smem, smem, hbm, hbm, hbm, hbm, hbm],
        out_specs=(vmem, vmem, vmem, vmem),
        scratch_shapes=[
            pltpu.VMEM((WIDTH, NBLK * BLOCK), BF16),
            pltpu.VMEM((TILES, SLICE, BLOCK), F32),
            pltpu.VMEM((ROWS, WIDTH), BF16),
            pltpu.VMEM((ROWS, WIDTH), BF16),
            pltpu.VMEM((TILES, SLICE, BLOCK), BF16),
            pltpu.VMEM((PLACES, SLICE, BLOCK), BF16),
            pltpu.VMEM((MOST,) + square, BF16),
            pltpu.VMEM((ROWS, WIDTH), BF16),
            pltpu.VMEM((PARTS, N_DP, LOT, WIDTH), BF16),
            pltpu.VMEM((PARTS, N_DP, LOT, WIDTH), BF16),
            pltpu.VMEM((2 * PER, ROWS, CHUNK), BF16),
            pltpu.VMEM((CHUNKS, GROUP, CHUNK), BF16),
            pltpu.VMEM((PLACES, 2, GROUP, CHUNK), BF16),
            pltpu.VMEM((MOST, 2, 2, ROWS, CHUNK), BF16),
            pltpu.VMEM((MOST, 2, 2, ROWS, CHUNK), BF16),
            pltpu.VMEM((PLACES, 2, GROUP, CHUNK), BF16),
            pltpu.VMEM((NBLK, 2, 2, GROUP, CHUNK), BF16),
            pltpu.VMEM((2, 2, 2, ROWS, CHUNK), BF16),
            pltpu.VMEM(square, F32),
            pltpu.VMEM(square, F32),
            pltpu.VMEM(square, BF16),
            pltpu.VMEM(square, BF16),
            pltpu.VMEM(square, BF16),
            pltpu.VMEM(square, BF16),
            dma((SIDE,)), dma((4,)), dma((PARTS,)), dma((PARTS,)),
            dma((PARTS, N_DP)), dma((PARTS, N_DP)), pltpu.SemaphoreType.REGULAR,
        ] + [dma((N_DP,))] * 12,
        compiler_params=pltpu.CompilerParams(
            collective_id=0, has_side_effects=True, vmem_limit_bytes=48 * 1024 * 1024),
        name="refresh",
    )(table, place, ns_counts[0], acts[0], grad_top, slopes[0], weights_t[0], running[0])
    return (backs[None], pre_acts[None], pre_grads[None], inverses[None, None])


def solution(mesh):
    in_specs = (
        P("section", None, "dp"),
        P(None, "dp"),
        P("section", "dp", None),
        P("section", None, "dp"),
        P("section", None, "dp", None),
        P("section", None),
        P("section", None),
    )
    out_specs = (
        P("section", None, "dp"),
        P("section", None, "dp"),
        P("section", None, "dp"),
        P("section", "dp", None, None, None),
    )
    return jax.shard_map(shards, mesh=mesh, in_specs=in_specs, out_specs=out_specs, check_vma=False)
```

time: 208 us -> 129 us (0.62)
  Pallas kernels: 198 us -> 118 us
    pallas_call x1, Pallas kernels: 198 us -> 118 us  [shards(): pl.pallas_call(kernel, out_shape=(flat, flat, flat, jax.ShapeDtypeStruct(...]
where the time goes in v2:
time: 129 us
  Pallas kernels  118 us (91%)
  local copies, waits for them, and re-layouts  7.8 us (6%)
  other arithmetic  2.33 us (2%)
    pallas_call x1, Pallas kernels, shards(): pl.pallas_call(kernel, out_shape=(flat, flat, flat, jax.ShapeDtypeStruct(...  118 us
    unnamed x14, local copies, waits for them, and re-layouts  7.8 us

profile of v2, /device:TPU:0, one launch (start us, length us, event | category | flops | bytes accessed | tf_op | source)
XLA Modules:
  0.0 128.6 jit_solution(9028855652463384704)
XLA Ops:
  0.6 0.9 convert_reduce_fusion
  1.5 0.7 multiply_add_fusion.place
  2.2 0.7 fusion.1
  2.9 0.1 select_reduce_fusion
  3.0 0.0 copy-start
  3.0 1.4 %copy-done = f32[1,24,32,512]{3,2,1,0:T(8,128)S(1)} copy-done((f32[1,24,32,512]{3,2,1,0:T(8,128)S(1)}, f32[1,24,32,512]{3,2,1,0:T(8,128)}, u32[]{:S(2)}) %copy-start) | copy-done | bytes 1572888
  4.4 0.0 copy-start.1
  4.4 0.9 copy-done.1
  5.3 0.0 copy-start.2
  5.3 0.9 copy-done.2
  6.2 0.0 copy-start.3
  6.2 0.9 copy-done.3
  7.1 0.0 copy-start.4
  7.1 0.7 copy-done.4
  7.7 117.9 %refresh.1 = (bf16[128,384]{1,0:T(8,128)(2,1)S(1)}, bf16[128,384]{1,0:T(8,128)(2,1)S(1)}, bf16[128,384]{1,0:T(8,128)(2,1)S(1)}, bf16[3,512,512]{2,1,0:T(8,128)(2,1)S(1)}) custom-call(s32[48]{0:T(128)S(1)} %broadcast_add_fusion.table, s32[24]{0:T(128)S(1)} %multiply_add_fusion.place, s32[24]{0:T(128)S(1)} %bitcast.24, bf16[128,384]{1,0:T(8,128)(2,1)S(1)} %bitcast.22, ...), custom_call_target="tpu_custom_call" | custom-call | tf_op jit(solution)/shard_map/refresh/pallas_call | solution.py:353
  125.6 0.6 copy.15
  126.2 0.6 copy.16
  126.9 0.6 copy.17
  127.5 1.1 copy.18
  (2 shorter events, 0.0 us)
Async XLA Ops:
  3.0 1.4 %copy-start = (f32[1,24,32,512]{3,2,1,0:T(8,128)S(1)}, f32[1,24,32,512]{3,2,1,0:T(8,128)}, u32[]{:S(2)}) copy-start(f32[1,24,32,512]{3,2,1,0:T(8,128)} %param.11) | copy-start | bytes 4718596
  4.4 0.9 copy-start.1
  5.3 0.9 copy-start.2
  6.2 0.9 copy-start.3
  7.1 0.7 copy-start.4
